TPU v7x, 32 devices: a whole 2x2x4 slice. The times are simulated.
32 devices in a mesh: pair: 16 (over z, y, x), vir: 2 (over core).
Axes of the slice: x: 2, y: 2, z: 4, core: 2. Of those that a mesh axis runs over, the one named last changes fastest.
Arguments:
- amplitudes: bfloat16 [40960, 1024], P('pair', 'vir'), may hold values from -6 to 6
- cycle_ints: bfloat16 [40960, 1024], P('pair', 'vir'), may hold values from -6 to 6
- int_rows: bfloat16 [1024, 1024], P('pair', 'vir'), may hold values from -6 to 6
- row_dest: int32 [1024, 2], P('pair'), may hold values from 0 to 15, all different within a row; in each aligned block of 64 rows (0 to 63, 64 to 127, ...) at most 16 rows name the same one
- vir_energy: float32 [1024], P('vir'), may hold values from 0.5 to 4
- occ_energy: float32 [40960], P('pair'), may hold values from -2 to -0.2
Outputs:
- residual: bfloat16 [40960, 1024], P('pair', 'vir')
Inputs may be any that keep to these rules, and one draw needn't show every extreme that they name: `row_dest`: each integral row names 2 different pair groups; among the 64 rows of one pair group no group is named more than 16 times, a bound that some block reaches.
All inputs are finite; a program needn't handle non-finite values.
Results may differ from a plain program's by a relative error of at most 0.008.
Values may be sent and summed in bfloat16 or wider, within the bound.
A program may use at most 64 MiB of HBM per device.

v0:
```python
import math
import jax
import jax.numpy as jnp
from jax import lax
from jax.sharding import PartitionSpec as P

SLOTS = 256


def dispatch(int_rows, row_dest, groups, capacity):
    rows = int_rows.shape[0]
    group = jnp.arange(groups, dtype=jnp.int32)
    member = jnp.any(row_dest[None, :, :] == group[:, None, None], axis=2)
    before = jnp.arange(rows)[:, None] < jnp.arange(rows)[None, :]
    rank = jnp.dot(
        member.astype(jnp.bfloat16), before.astype(jnp.bfloat16), preferred_element_type=jnp.float32
    ).astype(jnp.int32)
    slot = jnp.arange(capacity, dtype=jnp.int32)
    select = member[:, None, :] & (rank[:, None, :] == slot[None, :, None])
    select = select.reshape(groups * capacity, rows).astype(int_rows.dtype)
    return jnp.dot(select, int_rows, preferred_element_type=jnp.float32).astype(int_rows.dtype)


def body(amplitudes, cycle_ints, int_rows, row_dest, vir_energy, occ_energy):
    groups = lax.axis_size("pair")
    row_count, local_width = amplitudes.shape
    full_width = local_width * lax.axis_size("vir")
    capacity = SLOTS // groups
    gathered = lax.all_gather(amplitudes, "vir", axis=1, tiled=True)
    cross_part = lax.dot_general(
        gathered, cycle_ints, (((0,), (0,)), ((), ())), preferred_element_type=jnp.float32
    )
    scale_cycle = math.sqrt(row_count * groups * full_width)
    cross_half = lax.psum((cross_part / scale_cycle).astype(jnp.bfloat16), "pair")
    outgoing = dispatch(int_rows, row_dest, groups, capacity)
    arrived = lax.all_to_all(
        outgoing.reshape(groups, capacity, local_width),
        "pair",
        split_axis=0,
        concat_axis=0,
        tiled=True,
    ).reshape(groups * capacity, local_width)
    chosen = lax.all_gather(arrived, "vir", axis=1, tiled=True)
    coefficient = lax.dot_general(
        gathered, chosen, (((1,), (1,)), ((), ())), preferred_element_type=jnp.float32
    ) / math.sqrt(full_width)
    ladder = jnp.dot(
        coefficient.astype(jnp.bfloat16), arrived, preferred_element_type=jnp.float32
    ) / math.sqrt(SLOTS)
    energy = (vir_energy[None, :] - occ_energy[:, None]) * amplitudes.astype(jnp.float32)
    cycle_term = jnp.dot(gathered, cross_half, preferred_element_type=jnp.float32)
    return (cycle_term + ladder + energy).astype(jnp.bfloat16)


def solution(mesh):
    return jax.shard_map(
        body,
        mesh=mesh,
        in_specs=(
            P("pair", "vir"),
            P("pair", "vir"),
            P("pair", "vir"),
            P("pair", None),
            P("vir"),
            P("pair"),
        ),
        out_specs=P("pair", "vir"),
        check_vma=False,
    )
```

profile of v0, /device:TPU:0, one launch (start us, length us, event | category | flops | bytes accessed | tf_op | source)
XLA Modules:
  0.0 178.0 jit_solution(11613272002490482271)
XLA Ops:
  6.5 0.0 copy-start
  6.5 0.0 all-gather.2.cloned.1.call-start
  6.5 0.7 all-gather.2.cloned.1.call-update
  7.3 0.0 all-reduce.2.cloned.1.call-start
  7.3 0.1 eq.39
  7.4 0.7 fusion.4
  8.1 0.0 copy-start.1
  8.1 18.8 %all-gather.2.cloned.1.call-done = bf16[2560,1024]{1,0:T(8,128)(2,1)} async-done(((bf16[2560,512]{1,0:T(8,128)(2,1)}), bf16[2560,1024]{1,0:T(8,128)(2,1)}) %all-gather.2.cloned.1.call-update) | async-done | bytes 5242896 | tf_op jit(solution)/shard_map/all_gather | solution.py:29
  26.9 0.0 copy-done
  26.9 6.4 %multiply_convert_fusion = bf16[1024,512]{1,0:T(8,128)(2,1)} fusion(bf16[2560,1024]{1,0:T(8,128)(2,1)} %all-gather.2.cloned.1.call-done, bf16[2560,512]{1,0:T(8,128)(2,1)S(1)} %copy-done), kind=kOutput, calls=%fused_computation.5 | convolution fusion | flops 2685403136 | bytes 8912896 | tf_op jit(solution)/shard_map/dot_general | solution.py:30
  33.3 0.0 all-reduce.2.cloned.1.call-update
  33.3 0.1 convolution_convert_fusion.1
  33.4 0.1 fusion.3
  33.5 0.0 copy-done.1
  33.5 0.9 convolution_convert_fusion
  34.4 6.8 %all-to-all-start = ((bf16[16,16,512]{2,1,0:T(8,128)(2,1)}), bf16[16,16,512]{2,1,0:T(8,128)(2,1)S(1)}, u32[]{:S(2)}, u32[]{:S(2)}) async-start(bf16[16,16,512]{2,1,0:T(8,128)(2,1)} %bitcast.3), calls=%async_computation | async-start | bytes 524288 | tf_op jit(solution)/shard_map/all_to_all | solution.py:36
  41.2 4.4 %copy.12 = bf16[2560,512]{0,1:T(8,128)(2,1)} copy(bf16[2560,512]{1,0:T(8,128)(2,1)} %param.6) | data formatting | bytes 5242880 | tf_op args[0]
  45.6 9.9 %all-to-all-done = bf16[16,16,512]{2,1,0:T(8,128)(2,1)S(1)} async-done(((bf16[16,16,512]{2,1,0:T(8,128)(2,1)}), bf16[16,16,512]{2,1,0:T(8,128)(2,1)S(1)}, u32[]{:S(2)}, u32[]{:S(2)}) %all-to-all-start) | async-done | bytes 262176 | tf_op jit(solution)/shard_map/all_to_all | solution.py:36
  55.5 2.2 %all_gather.7 = bf16[256,1024]{1,0:T(8,128)(2,1)S(1)} all-gather(bf16[256,512]{1,0:T(8,128)(2,1)S(1)} %bitcast.24), channel_id=1, replica_groups=mesh['pair'=16,'vir'=2] {'vir'}, dimensions={1}, use_global_device_ids=true | all-gather | bytes 786432 | tf_op jit(solution)/shard_map/all_gather | solution.py:43
  57.7 0.0 copy-start.2
  57.7 0.0 copy-start.3
  57.7 92.0 %all-reduce.2.cloned.1.call-done = bf16[1024,512]{1,0:T(8,128)(2,1)} async-done(((bf16[1024,512]{1,0:T(8,128)(2,1)}), bf16[1024,512]{1,0:T(8,128)(2,1)}) %all-reduce.2.cloned.1.call-update) | async-done | bytes 1048592 | tf_op jit(solution)/shard_map/psum | solution.py:34
  149.7 8.1 %fusion.6 = f32[512,2560]{1,0:T(8,128)} fusion(bf16[1024,512]{1,0:T(8,128)(2,1)} %all-reduce.2.cloned.1.call-done, bf16[2560,1024]{1,0:T(8,128)(2,1)} %all-gather.2.cloned.1.call-done), kind=kOutput, calls=%fused_computation.14 | convolution fusion | flops 2684354560 | bytes 11534336 | tf_op jit(solution)/shard_map/dot_general | solution.py:51
  157.8 0.0 copy-done.2
  157.8 0.0 copy-done.3
  157.8 9.0 %fusion.1 = bf16[2560,512]{0,1:T(8,128)(2,1)} fusion(f32[512,2560]{1,0:T(8,128)} %fusion.6, bf16[2560,512]{0,1:T(8,128)(2,1)} %copy.12, bf16[256,512]{1,0:T(8,128)(2,1)S(1)} %bitcast.25, f32[2560]{0:T(1024)S(1)} %copy-done.2, f32[512]{0:T(512)S(1)} %copy-done.3, bf16[256,1024]{1,0:T(8,128)(2,1)S(1)} %all_gather.7, ...), kind=kOutput, calls=%fused_computation.2 | convolution fusion | flops 2023751680 | bytes 16527360 | tf_op jit(solution)/shard_map/dot_general | solution.py:47
  166.8 4.4 %copy.13 = bf16[2560,512]{1,0:T(8,128)(2,1)} copy(bf16[2560,512]{0,1:T(8,128)(2,1)} %fusion.1) | data formatting | bytes 5242880 | tf_op jit(solution)/shard_map/convert_element_type | solution.py:52
  (1 shorter events, 0.0 us)
Async XLA Ops:
  6.5 20.3 %copy-start = (bf16[2560,512]{1,0:T(8,128)(2,1)S(1)}, bf16[2560,512]{1,0:T(8,128)(2,1)}, u32[]{:S(2)}) copy-start(bf16[2560,512]{1,0:T(8,128)(2,1)} %param.7) | copy-start | bytes 7864324
  6.5 20.3 %all-gather.2.cloned.1.call-start = ((), (), s32[]{:S(2)}) async-start(), calls=%async_computation.1 | async-start | bytes 7864320 | tf_op jit(solution)/shard_map/all_gather | solution.py:29
  7.3 142.4 %all-reduce.2.cloned.1.call-start = ((), (), s32[]{:S(2)}) async-start(), calls=%async_computation.2 | async-start | bytes 2097152 | tf_op jit(solution)/shard_map/psum | solution.py:34
  8.1 25.4 %copy-start.1 = (bf16[64,512]{1,0:T(8,128)(2,1)S(1)}, bf16[64,512]{1,0:T(8,128)(2,1)}, u32[]{:S(2)}) copy-start(bf16[64,512]{1,0:T(8,128)(2,1)} %param.8) | copy-start | bytes 196612
  34.4 21.1 %all-to-all-start = ((bf16[16,16,512]{2,1,0:T(8,128)(2,1)}), bf16[16,16,512]{2,1,0:T(8,128)(2,1)S(1)}, u32[]{:S(2)}, u32[]{:S(2)}) async-start(bf16[16,16,512]{2,1,0:T(8,128)(2,1)} %bitcast.3), calls=%async_computation | async-start | bytes 524288 | tf_op jit(solution)/shard_map/all_to_all | solution.py:36
  57.7 100.1 %copy-start.2 = (f32[2560]{0:T(1024)S(1)}, f32[2560]{0:T(1024)}, u32[]{:S(2)}) copy-start(f32[2560]{0:T(1024)} %param.11) | copy-start | bytes 30724
  57.7 100.1 %copy-start.3 = (f32[512]{0:T(512)S(1)}, f32[512]{0:T(512)}, u32[]{:S(2)}) copy-start(f32[512]{0:T(512)} %param.10) | copy-start | bytes 6148
Sparse Core Ops, SparseCore 0:
  8.9 17.9 all-gather.1
  33.4 116.2 all-reduce.1
where the time goes:
time: 178 us
  waiting for transfers between devices  121 us (68%)
  matrix products  24.5 us (14%)
  between operations  13.4 us (8%)
  local copies, waits for them, and re-layouts  8.86 us (5%)
  starting transfers between devices  6.82 us (4%)
  blocking collectives  2.17 us (1%)
    psum x1, waiting for transfers between devices, body(): lax.psum((cross_part / scale_cycle).astype(jnp.bfloat16), 'pair')  92 us
    all_gather x1, waiting for transfers between devices, body(): gathered = lax.all_gather(amplitudes, 'vir', axis=1, tiled=True)  18.8 us
    all_to_all x1, waiting for transfers between devices, body(): lax.all_to_all(outgoing.reshape(groups, capacity, local_width), 'pair', s...  9.9 us
    dot_general x1, matrix products, body(): jnp.dot(coefficient.astype(jnp.bfloat16), arrived, preferred_element_type...  9.01 us
    dot_general x1, matrix products, body(): jnp.dot(gathered, cross_half, preferred_element_type=jnp.float32)  8.08 us
    all_to_all x1, starting transfers between devices, body(): lax.all_to_all(outgoing.reshape(groups, capacity, local_width), 'pair', s...  6.78 us
    dot_general x1, matrix products, body(): lax.dot_general(gathered, cycle_ints, (((0,), (0,)), ((), ())), preferred...  6.4 us
    unnamed x9, local copies, waits for them, and re-layouts  4.4 us
  transfers between devices with their start and end apart: 3, of which 3 were waited for; matrix products, arithmetic and copies ran while one was open for 4% of the time, Pallas kernels for 0%

commit v1 on v0

--- a/solution.py
+++ b/solution.py
@@ -31,7 +31,8 @@
         gathered, cycle_ints, (((0,), (0,)), ((), ())), preferred_element_type=jnp.float32
     )
     scale_cycle = math.sqrt(row_count * groups * full_width)
-    cross_half = lax.psum((cross_part / scale_cycle).astype(jnp.bfloat16), "pair")
+    put_domain_in = lambda view: jnp.sum(jax.lax.all_gather(view, axis_name="pair"), 0)
+    cross_half = put_domain_in((cross_part / scale_cycle).astype(jnp.bfloat16))
     outgoing = dispatch(int_rows, row_dest, groups, capacity)
     arrived = lax.all_to_all(
         outgoing.reshape(groups, capacity, local_width),

time: 178 us -> 268 us (1.51)
  waiting for transfers between devices: 121 us -> 201 us
  other arithmetic: 0.8 us -> 10 us
    all_gather x0 -> x1, waiting for transfers between devices: none -> 172 us  [body(): jax.lax.all_gather(view, axis_name='pair')]
    psum x1 -> x0, waiting for transfers between devices: 92 us -> none  [body(): lax.psum((cross_part / scale_cycle).astype(jnp.bfloat16), 'pair')]
    reduce_sum x0 -> x1, other arithmetic: none -> 9.92 us  [body(): jnp.sum(jax.lax.all_gather(view, axis_name='pair'), 0)]
  transfers between devices with their start and end apart: 3 -> 3, of which waited for: 3 -> 3; matrix products, arithmetic and copies ran while one was open for 4% -> 2% of each run, Pallas kernels for 0% -> 0%
where the time goes in v1:
time: 268 us; the launch traced here: 267 us
  waiting for transfers between devices  201 us (75%)
  matrix products  24.5 us (9%)
  between operations  13.5 us (5%)
  other arithmetic  10 us (4%)
  local copies, waits for them, and re-layouts  9.01 us (3%)
  starting transfers between devices  6.82 us (3%)
    all_gather x1, waiting for transfers between devices, body(): jax.lax.all_gather(view, axis_name='pair')  172 us
    all_gather x1, waiting for transfers between devices, body(): gathered = lax.all_gather(amplitudes, 'vir', axis=1, tiled=True)  19.5 us
    reduce_sum x1, other arithmetic, body(): jnp.sum(jax.lax.all_gather(view, axis_name='pair'), 0)  9.92 us
    all_to_all x1, waiting for transfers between devices, body(): lax.all_to_all(outgoing.reshape(groups, capacity, local_width), 'pair', s...  9.33 us
    dot_general x1, matrix products, body(): jnp.dot(coefficient.astype(jnp.bfloat16), arrived, preferred_element_type...  8.98 us
    dot_general x1, matrix products, body(): jnp.dot(gathered, cross_half, preferred_element_type=jnp.float32)  8.07 us
    all_to_all x1, starting transfers between devices, body(): lax.all_to_all(outgoing.reshape(groups, capacity, local_width), 'pair', s...  6.78 us
    dot_general x1, matrix products, body(): lax.dot_general(gathered, cycle_ints, (((0,), (0,)), ((), ())), preferred...  6.4 us
  transfers between devices with their start and end apart: 3, of which 3 were waited for; matrix products, arithmetic and copies ran while one was open for 2% of the time, Pallas kernels for 0%

profile of v1, /device:TPU:0, one launch (start us, length us, event | category | flops | bytes accessed | tf_op | source)
XLA Modules:
  0.0 267.2 jit_solution(10140457295716276871)
XLA Ops:
  6.5 0.0 copy-start
  6.5 0.0 all-gather.4.cloned.1.call-start
  6.5 0.7 all-gather.4.cloned.1.call-update
  7.3 0.0 copy-start.2
  7.3 0.0 copy-start.1
  7.3 0.0 all-gather.6.cloned.1.call-start
  7.3 19.5 %all-gather.4.cloned.1.call-done = bf16[2560,1024]{1,0:T(8,128)(2,1)} async-done(((bf16[2560,512]{1,0:T(8,128)(2,1)}), bf16[2560,1024]{1,0:T(8,128)(2,1)}) %all-gather.4.cloned.1.call-update) | async-done | bytes 5242896 | tf_op jit(solution)/shard_map/all_gather | solution.py:29
  26.9 0.0 copy-done
  26.9 6.4 %multiply_convert_fusion = bf16[1024,512]{1,0:T(8,128)(2,1)} fusion(bf16[2560,1024]{1,0:T(8,128)(2,1)} %all-gather.4.cloned.1.call-done, bf16[2560,512]{1,0:T(8,128)(2,1)S(1)} %copy-done), kind=kOutput, calls=%fused_computation.5 | convolution fusion | flops 2685403136 | bytes 8912896 | tf_op jit(solution)/shard_map/dot_general | solution.py:30
  33.3 0.0 all-gather.6.cloned.1.call-update
  33.3 0.1 eq.39
  33.4 0.0 copy-done.2
  33.4 0.1 convolution_convert_fusion.1
  33.5 0.1 fusion.3
  33.6 0.0 copy-done.1
  33.6 0.9 convolution_convert_fusion
  34.5 6.8 %all-to-all-start = ((bf16[16,16,512]{2,1,0:T(8,128)(2,1)}), bf16[16,16,512]{2,1,0:T(8,128)(2,1)S(1)}, u32[]{:S(2)}, u32[]{:S(2)}) async-start(bf16[16,16,512]{2,1,0:T(8,128)(2,1)} %bitcast.4), calls=%async_computation | async-start | bytes 524288 | tf_op jit(solution)/shard_map/all_to_all | solution.py:37
  41.3 4.5 %copy.12 = bf16[2560,512]{0,1:T(8,128)(2,1)} copy(bf16[2560,512]{1,0:T(8,128)(2,1)} %param.6) | data formatting | bytes 5242880 | tf_op args[0]
  45.9 9.3 %all-to-all-done = bf16[16,16,512]{2,1,0:T(8,128)(2,1)S(1)} async-done(((bf16[16,16,512]{2,1,0:T(8,128)(2,1)}), bf16[16,16,512]{2,1,0:T(8,128)(2,1)S(1)}, u32[]{:S(2)}, u32[]{:S(2)}) %all-to-all-start) | async-done | bytes 262176 | tf_op jit(solution)/shard_map/all_to_all | solution.py:37
  55.2 2.2 all_gather.15
  57.4 171.7 %all-gather.6.cloned.1.call-done = bf16[16384,512]{1,0:T(8,128)(2,1)} async-done(((bf16[1024,512]{1,0:T(8,128)(2,1)}), bf16[16384,512]{1,0:T(8,128)(2,1)}) %all-gather.6.cloned.1.call-update) | async-done | bytes 16777232 | tf_op jit(solution)/shard_map/all_gather | solution.py:34
  229.0 9.9 %reduce_sum.12 = bf16[1024,512]{1,0:T(8,128)(2,1)} reduce(bf16[16,1024,512]{2,1,0:T(8,128)(2,1)} %bitcast.25, bf16[]{:T(256)} %constant.10.clone.1), dimensions={0}, to_apply=%region_0.0 | reduce | flops 7864320 | bytes 17825794 | tf_op jit(solution)/shard_map/reduce_sum | solution.py:34
  238.9 0.0 copy-start.3
  238.9 0.0 copy-start.4
  238.9 8.1 %fusion.6 = f32[512,2560]{1,0:T(8,128)} fusion(bf16[1024,512]{1,0:T(8,128)(2,1)} %reduce_sum.12, bf16[2560,1024]{1,0:T(8,128)(2,1)} %all-gather.4.cloned.1.call-done), kind=kOutput, calls=%fused_computation.14 | convolution fusion | flops 2684354560 | bytes 11534336 | tf_op jit(solution)/shard_map/dot_general | solution.py:52
  247.0 0.0 copy-done.3
  247.0 0.0 copy-done.4
  247.0 9.0 %fusion.1 = bf16[2560,512]{0,1:T(8,128)(2,1)} fusion(f32[512,2560]{1,0:T(8,128)} %fusion.6, bf16[2560,512]{0,1:T(8,128)(2,1)} %copy.12, bf16[256,512]{1,0:T(8,128)(2,1)S(1)} %bitcast.27, f32[2560]{0:T(1024)S(1)} %copy-done.3, f32[512]{0:T(512)S(1)} %copy-done.4, bf16[256,1024]{1,0:T(8,128)(2,1)S(1)} %all_gather.15, ...), kind=kOutput, calls=%fused_computation.2 | convolution fusion | flops 2023751680 | bytes 16527360 | tf_op jit(solution)/shard_map/dot_general | solution.py:48
  256.0 4.4 %copy.13 = bf16[2560,512]{1,0:T(8,128)(2,1)} copy(bf16[2560,512]{0,1:T(8,128)(2,1)} %fusion.1) | data formatting | bytes 5242880 | tf_op jit(solution)/shard_map/convert_element_type | solution.py:53
  (2 shorter events, 0.0 us)
Async XLA Ops:
  6.5 20.3 %copy-start = (bf16[2560,512]{1,0:T(8,128)(2,1)S(1)}, bf16[2560,512]{1,0:T(8,128)(2,1)}, u32[]{:S(2)}) copy-start(bf16[2560,512]{1,0:T(8,128)(2,1)} %param.7) | copy-start | bytes 7864324
  6.5 20.3 %all-gather.4.cloned.1.call-start = ((), (), s32[]{:S(2)}) async-start(), calls=%async_computation.1 | async-start | bytes 7864320 | tf_op jit(solution)/shard_map/all_gather | solution.py:29
  7.3 26.1 %copy-start.2 = (s32[64,2]{0,1:T(2,128)S(1)}, s32[64,2]{0,1:T(2,128)}, u32[]{:S(2)}) copy-start(s32[64,2]{0,1:T(2,128)} %param.9) | copy-start | bytes 1540
  7.3 26.4 %copy-start.1 = (bf16[64,512]{1,0:T(8,128)(2,1)S(1)}, bf16[64,512]{1,0:T(8,128)(2,1)}, u32[]{:S(2)}) copy-start(bf16[64,512]{1,0:T(8,128)(2,1)} %param.8) | copy-start | bytes 196612
  7.3 221.7 %all-gather.6.cloned.1.call-start = ((), (), s32[]{:S(2)}) async-start(), calls=%async_computation.2 | async-start | bytes 17825792 | tf_op jit(solution)/shard_map/all_gather | solution.py:34
  34.5 20.6 %all-to-all-start = ((bf16[16,16,512]{2,1,0:T(8,128)(2,1)}), bf16[16,16,512]{2,1,0:T(8,128)(2,1)S(1)}, u32[]{:S(2)}, u32[]{:S(2)}) async-start(bf16[16,16,512]{2,1,0:T(8,128)(2,1)} %bitcast.4), calls=%async_computation | async-start | bytes 524288 | tf_op jit(solution)/shard_map/all_to_all | solution.py:37
  238.9 8.1 %copy-start.3 = (f32[2560]{0:T(1024)S(1)}, f32[2560]{0:T(1024)}, u32[]{:S(2)}) copy-start(f32[2560]{0:T(1024)} %param.11) | copy-start | bytes 30724
  238.9 8.1 %copy-start.4 = (f32[512]{0:T(512)S(1)}, f32[512]{0:T(512)}, u32[]{:S(2)}) copy-start(f32[512]{0:T(512)} %param.10) | copy-start | bytes 6148
Sparse Core Ops, SparseCore 0:
  8.9 17.9 all-gather.3
  33.4 195.5 all-gather.5
